TPU v7x, 1024 devices: a whole 8x8x8 slice. The times are simulated.
1024 devices in a mesh: grp: 16 (over z, core), blk: 64 (over y, x).
Axes of the slice: x: 8, y: 8, z: 8, core: 2. Of those that a mesh axis runs over, the one named last changes fastest.
Arguments:
- features: bfloat16 [1048576, 128], P(('grp', 'blk')), may hold values from -6 to 6
- cotangent: bfloat16 [1048576, 256], P(('grp', 'blk')), may hold values from -15 to 15
- self_weight: bfloat16 [128, 256], replicated, may hold values from -0.5 to 0.5
- mean_weight: bfloat16 [128, 256], replicated, may hold values from -0.5 to 0.5
- bias_term: float32 [256], replicated, may hold values from -3 to 3
- edge_source: int32 [16, 64, 64, 128], P('grp', 'blk'), may hold values from 0 to 1023
- edge_target: int32 [16, 64, 64, 128], P('grp', 'blk'), may hold values from 0 to 3071
- block_counts: int32 [16, 64], P('grp', 'blk'), may hold values from 1 to 64
- receive_rows: int32 [16, 64, 16, 128], P('grp', 'blk'), may hold values from 0 to 1007
Outputs:
- activation: bfloat16 [1048576, 256], P(('grp', 'blk'))
- feature_grad: bfloat16 [1048576, 128], P(('grp', 'blk'))
- self_grad: float32 [128, 256], replicated
- mean_grad: float32 [128, 256], replicated
- bias_grad: float32 [256], replicated
All inputs are finite; a program needn't handle non-finite values.
Results may differ from a plain program's by a relative error of at most 0.0055.
Values may be sent and summed in bfloat16 or wider, within the bound.
A program may use at most 32 MiB of HBM per device.

v0:
```python
import jax
import jax.numpy as jnp
from jax import lax
from jax.sharding import PartitionSpec as P

HUB_DEV = 16


def layer_pass(inputs, neighbour_mean, upstream, self_weight, mean_weight, bias_term):
    pre_act = (
        jnp.dot(inputs, self_weight, preferred_element_type=jnp.float32)
        + jnp.dot(neighbour_mean, mean_weight, preferred_element_type=jnp.float32)
        + bias_term
    )
    sigmoid_part = jax.nn.sigmoid(pre_act)
    activation = (pre_act * sigmoid_part).astype(jnp.bfloat16)
    pre_grad = (
        upstream.astype(jnp.float32) * sigmoid_part * (1.0 + pre_act * (1.0 - sigmoid_part))
    ).astype(jnp.bfloat16)
    return (activation, pre_grad)


def back_project(pre_grad, weight_matrix):
    return lax.dot_general(
        pre_grad, weight_matrix, (((1,), (1,)), ((), ())), preferred_element_type=jnp.float32
    )


def edge_total(source_table, take_index, put_index, live_blocks, buckets):
    blocks, width_rows = take_index.shape
    usable = jnp.arange(blocks, dtype=jnp.int32)[:, None] < live_blocks
    usable = jnp.broadcast_to(usable, take_index.shape).reshape(-1)
    target = jnp.where(usable, put_index.reshape(-1), buckets)
    totals = jax.ops.segment_sum(
        source_table[take_index.reshape(-1)].astype(jnp.float32), target, buckets + 1
    )
    tallies = jax.ops.segment_sum(usable.astype(jnp.float32), target, buckets + 1)
    return (totals[:buckets], tallies[:buckets])


def local(
    features,
    cotangent,
    self_weight,
    mean_weight,
    bias_term,
    edge_source,
    edge_target,
    block_counts,
    receive_rows,
):
    groups = lax.axis_size("grp")
    vertices, feature_width = features.shape
    capacity = receive_rows.shape[3]
    slot_count = groups * capacity
    hub_count = HUB_DEV * lax.axis_size("blk")
    bucket_count = slot_count + hub_count
    regular = vertices - HUB_DEV
    sources = edge_source.reshape(-1, edge_source.shape[3])
    targets = edge_target.reshape(-1, edge_target.shape[3])
    live_blocks = block_counts.reshape(())
    totals, tallies = edge_total(features, sources, targets, live_blocks, bucket_count)
    partials = totals[:slot_count].astype(jnp.bfloat16).reshape(groups, capacity, feature_width)
    slot_tally = tallies[:slot_count].astype(jnp.bfloat16).reshape(groups, capacity)
    arrived, arrived_tally = (
        lax.all_to_all(partials, "grp", split_axis=0, concat_axis=0, tiled=True),
        lax.all_to_all(slot_tally, "grp", split_axis=0, concat_axis=0, tiled=True),
    )
    row_index = receive_rows.reshape(-1)
    summed = jax.ops.segment_sum(
        arrived.reshape(slot_count, feature_width).astype(jnp.float32), row_index, regular
    )
    degree = jax.ops.segment_sum(
        arrived_tally.reshape(slot_count).astype(jnp.float32), row_index, regular
    )
    hub_part = totals[slot_count:]
    hub_tally = tallies[slot_count:]
    own_sums, own_degree = (
        lax.psum_scatter(hub_part, "blk", scatter_dimension=0, tiled=True),
        lax.psum_scatter(hub_tally, "blk", scatter_dimension=0, tiled=True),
    )
    summed = jnp.concatenate([summed, own_sums], 0)
    degree = jnp.concatenate([degree, own_degree], 0)
    divisor = jnp.maximum(degree, 1.0)[:, None]
    neighbour_mean = (summed / divisor).astype(jnp.bfloat16)
    activation, pre_grad = layer_pass(
        features, neighbour_mean, cotangent, self_weight, mean_weight, bias_term
    )
    contract_rows = (((0,), (0,)), ((), ()))
    self_part = lax.dot_general(
        features, pre_grad, contract_rows, preferred_element_type=jnp.float32
    )
    mean_part = lax.dot_general(
        neighbour_mean, pre_grad, contract_rows, preferred_element_type=jnp.float32
    )
    bias_part = jnp.sum(pre_grad.astype(jnp.float32), axis=0)
    mean_rows = (back_project(pre_grad, mean_weight) / divisor).astype(jnp.bfloat16)
    returned = lax.all_to_all(
        mean_rows[row_index].reshape(groups, capacity, feature_width),
        "grp",
        split_axis=0,
        concat_axis=0,
        tiled=True,
    )
    hub_back = lax.all_gather(mean_rows[regular:], "blk", axis=0, tiled=True)
    grad_table = jnp.concatenate([returned.reshape(slot_count, feature_width), hub_back], 0)
    edge_grads, unused_tally = edge_total(grad_table, targets, sources, live_blocks, vertices)
    feature_grad = (back_project(pre_grad, self_weight) + edge_grads).astype(jnp.bfloat16)
    self_grad, mean_grad, bias_grad = lax.psum((self_part, mean_part, bias_part), ("grp", "blk"))
    return (activation, feature_grad, self_grad, mean_grad, bias_grad)


def solution(mesh):
    placed = (
        P(("grp", "blk"), None),
        P(("grp", "blk"), None),
        P(),
        P(),
        P(),
        P("grp", "blk", None, None),
        P("grp", "blk", None, None),
        P("grp", "blk"),
        P("grp", "blk", None, None),
    )
    return jax.shard_map(
        local,
        mesh=mesh,
        in_specs=placed,
        out_specs=(P(("grp", "blk"), None), P(("grp", "blk"), None), P(), P(), P()),
        check_vma=False,
    )
```

profile of v0, /device:TPU:1, one launch (start us, length us, event | category | flops | bytes accessed | tf_op | source)
XLA Modules:
  0.0 733.0 jit_solution(18178755908287800555)
XLA Ops:
  8.0 0.9 compare_select_fusion
  8.9 50.1 %scatter_custom_fusion.2 = f32[3073]{0:T(1024)S(1)} fusion(s32[8192]{0:T(1024)S(1)} %bitcast.50, f32[8192]{0:T(1024)S(1)} %broadcast_bitcast_fusion, f32[]{:T(128)} %constant.5.clone.1), kind=kCustom, calls=%fused_computation.42 | custom fusion | flops 8192 | bytes 12296 | tf_op jit(solution)/shard_map/scatter-add | solution.py:37
  59.7 19.2 %all-to-all-start.1 = ((bf16[16,1,128]{2,1,0:T(2,128)(2,1)}), bf16[16,1,128]{2,1,0:T(2,128)(2,1)S(1)}, u32[]{:S(2)}, u32[]{:S(2)}) async-start(bf16[16,1,128]{2,1,0:T(2,128)(2,1)} %copy.16), calls=%async_computation.1 | async-start | bytes 16384 | tf_op jit(solution)/shard_map/all_to_all | solution.py:67
  78.9 75.4 %scatter_custom_fusion = f32[3073,128]{1,0:T(8,128)S(1)} fusion(s32[8192]{0:T(1024)S(1)} %bitcast.51, f32[]{:T(128)} %constant.5.clone.1, bf16[1024,128]{1,0:T(8,128)(2,1)S(1)} %copy-done, s32[8192]{0:T(1024)S(1)} %broadcast_clamp_fusion.1), kind=kCustom, calls=%fused_computation.10 | custom fusion | flops 2097152 | bytes 1868292 | tf_op jit(solution)/shard_map/scatter-add | solution.py:34
  154.4 0.8 slice.39
  155.2 0.9 slice.57
  156.1 1.3 dynamic-slice
  158.0 115.3 %all-reduce.1 = f32[1024]{0:T(1024)S(1)} all-reduce(f32[1024]{0:T(1024)S(1)} %slice.41), channel_id=3, replica_groups=mesh['grp'=16,'blk'=64] {'blk'}, use_global_device_ids=true, to_apply=%region_5.6.clone | all-reduce | flops 1024 | bytes 8192
  273.4 39.0 %all-to-all-start = ((bf16[16,128,128]{2,1,0:T(8,128)(2,1)}), bf16[16,128,128]{2,1,0:T(8,128)(2,1)S(1)}, u32[]{:S(2)}, u32[]{:S(2)}) async-start(bf16[16,128,128]{2,1,0:T(8,128)(2,1)} %bitcast.6), calls=%async_computation | async-start | bytes 1048576 | tf_op jit(solution)/shard_map/all_to_all | solution.py:66
  312.8 14.7 %scatter_custom_fusion.3 = f32[1008]{0:T(1024)S(1)} fusion(s32[2048]{0:T(1024)S(1)} %bitcast.54, f32[2048]{0:T(1024)S(1)} %bitcast.56, f32[]{:T(128)} %constant.5.clone.1), kind=kCustom, calls=%fused_computation.47 | custom fusion | flops 2048 | bytes 4036 | tf_op jit(solution)/shard_map/scatter-add | solution.py:73
  327.6 0.7 constant_dynamic-slice_fusion
  328.3 1.5 all-to-all-done
  329.7 11.6 %scatter_custom_fusion.1 = f32[1008,128]{1,0:T(8,128)S(1)} fusion(s32[2048]{0:T(1024)S(1)} %bitcast.55, bf16[2048,128]{1,0:T(8,128)(2,1)S(1)} %bitcast.44, f32[]{:T(128)} %constant.5.clone.1), kind=kCustom, calls=%fused_computation.20 | custom fusion | flops 524288 | bytes 1040388 | tf_op jit(solution)/shard_map/scatter-add | solution.py:70
  341.6 2.5 convert_reduce_fusion
  344.4 8.0 %gather_fusion = bf16[2048,128]{1,0:T(8,128)(2,1)} fusion(bf16[1024,128]{1,0:T(8,128)(2,1)S(1)} %fusion.6, s32[2048]{0:T(1024)S(1)} %broadcast_clamp_fusion.2), kind=kCustom, calls=%fused_computation.1 | custom fusion | bytes 1056768 | tf_op jit(solution)/shard_map/gather | solution.py:99
  352.4 6.1 all-to-all-start.2
  358.5 0.9 fusion.22
  359.5 1.0 convolution_bitcast_fusion
  360.5 116.1 %psum.23 = f32[256]{0:T(256)} all-reduce(f32[256]{0:T(256)S(1)} %get-tuple-element.22), channel_id=1, replica_groups=mesh['grp'=16,'blk'=64] {'grp','blk'}, use_global_device_ids=true, to_apply=%region_10.11 | all-reduce | flops 256 | bytes 2048 | tf_op jit(solution)/shard_map/psum | solution.py:109
  476.6 35.6 %all_gather.3 = bf16[1024,128]{1,0:T(8,128)(2,1)S(1)} all-gather(bf16[16,128]{1,0:T(8,128)(2,1)S(1)} %slice.42), channel_id=1, replica_groups=mesh['grp'=16,'blk'=64] {'blk'}, dimensions={0}, use_global_device_ids=true | all-gather | bytes 266240 | tf_op jit(solution)/shard_map/all_gather | solution.py:105
  512.2 135.4 %all-reduce.8.cloned.1.call-done = (f32[128,256]{0,1:T(8,128)}, f32[128,256]{1,0:T(8,128)}) async-done(((f32[128,256]{0,1:T(8,128)}, f32[128,256]{1,0:T(8,128)}), (f32[128,256]{0,1:T(8,128)}, f32[128,256]{1,0:T(8,128)})) %all-reduce.8.cloned.1.call-update) | async-done | bytes 262160 | tf_op jit(solution)/shard_map/psum | solution.py:109
  647.6 1.7 copy.17
  649.3 75.2 %scatter_custom_fusion.4 = f32[1025,128]{1,0:T(8,128)S(1)} fusion(s32[8192]{0:T(1024)S(1)} %bitcast.49, f32[]{:T(128)} %constant.5.clone.1, bf16[3072,128]{1,0:T(8,128)(2,1)S(1)} %pad_maximum_fusion, s32[8192]{0:T(1024)S(1)} %broadcast_clamp_fusion), kind=kCustom, calls=%fused_computation.8 | custom fusion | flops 2097152 | bytes 1344004 | tf_op jit(solution)/shard_map/scatter-add | solution.py:34
  724.5 1.0 fusion.5
  (38 shorter events, 2.6 us)
Async XLA Ops:
  7.2 71.7 %copy-start = (bf16[1024,128]{1,0:T(8,128)(2,1)S(1)}, bf16[1024,128]{1,0:T(8,128)(2,1)}, u32[]{:S(2)}) copy-start(bf16[1024,128]{1,0:T(8,128)(2,1)} %param.9) | copy-start | bytes 786436
  59.7 213.7 %all-to-all-start.1 = ((bf16[16,1,128]{2,1,0:T(2,128)(2,1)}), bf16[16,1,128]{2,1,0:T(2,128)(2,1)S(1)}, u32[]{:S(2)}, u32[]{:S(2)}) async-start(bf16[16,1,128]{2,1,0:T(2,128)(2,1)} %copy.16), calls=%async_computation.1 | async-start | bytes 16384 | tf_op jit(solution)/shard_map/all_to_all | solution.py:67
  78.8 248.7 %all-reduce.6.cloned.1.call-start = ((), (), s32[]{:S(2)}) async-start(), calls=%async_computation.3 | async-start | bytes 1048576
  155.2 157.2 %copy-start.3 = (s32[1,1,16,128]{3,2,1,0:T(8,128)S(1)}, s32[1,1,16,128]{3,2,1,0:T(8,128)}, u32[]{:S(2)}) copy-start(s32[1,1,16,128]{3,2,1,0:T(8,128)} %param.17) | copy-start | bytes 24580
  155.2 157.3 %copy-start.1 = (bf16[128,256]{1,0:T(8,128)(2,1)S(1)}, bf16[128,256]{1,0:T(8,128)(2,1)}, u32[]{:S(2)}) copy-start(bf16[128,256]{1,0:T(8,128)(2,1)} %param.11) | copy-start | bytes 196612
  273.4 56.4 %all-to-all-start = ((bf16[16,128,128]{2,1,0:T(8,128)(2,1)}), bf16[16,128,128]{2,1,0:T(8,128)(2,1)S(1)}, u32[]{:S(2)}, u32[]{:S(2)}) async-start(bf16[16,128,128]{2,1,0:T(8,128)(2,1)} %bitcast.6), calls=%async_computation | async-start | bytes 1048576 | tf_op jit(solution)/shard_map/all_to_all | solution.py:66
  312.5 29.1 %copy-start.4 = (bf16[128,256]{1,0:T(8,128)(2,1)S(1)}, bf16[128,256]{1,0:T(8,128)(2,1)}, u32[]{:S(2)}) copy-start(bf16[128,256]{1,0:T(8,128)(2,1)} %param.12) | copy-start | bytes 196612
  312.5 29.1 %copy-start.5 = (f32[256]{0:T(256)S(1)}, f32[256]{0:T(256)}, u32[]{:S(2)}) copy-start(f32[256]{0:T(256)} %param.13) | copy-start | bytes 3076
  352.4 296.9 %all-to-all-start.2 = ((bf16[16,128,128]{2,1,0:T(8,128)(2,1)}), bf16[16,128,128]{2,1,0:T(8,128)(2,1)S(1)}, u32[]{:S(2)}, u32[]{:S(2)}) async-start(bf16[16,128,128]{2,1,0:T(8,128)(2,1)} %bitcast.14), calls=%async_computation.2 | async-start | bytes 1048576 | tf_op jit(solution)/shard_map/all_to_all | solution.py:98
  358.5 289.1 %all-reduce.8.cloned.1.call-start = ((), (), s32[]{:S(2)}) async-start(), calls=%async_computation.4 | async-start | bytes 524288 | tf_op jit(solution)/shard_map/psum | solution.py:109
  649.3 76.2 %copy-start.2 = (f32[128,256]{1,0:T(8,128)S(1)}, f32[128,256]{1,0:T(8,128)}, u32[]{:S(2)}) copy-start(f32[128,256]{1,0:T(8,128)} %get-tuple-element.36) | copy-start | bytes 393220
Sparse Core Ops, SparseCore 0:
  155.3 167.2 all-reduce.5
  365.6 281.9 all-reduce.7
where the time goes:
time: 736 us; the launch traced here: 733 us
  blocking collectives  267 us (36%)
  other arithmetic  228 us (31%)
  waiting for transfers between devices  137 us (19%)
  starting transfers between devices  64.3 us (9%)
  between operations  15.6 us (2%)
  local copies, waits for them, and re-layouts  14.8 us (2%)
    scatter-add x2, other arithmetic, edge_total(): jax.ops.segment_sum(source_table[take_index.reshape(-1)].astype(jnp.float...  151 us
    psum x1, waiting for transfers between devices, local(): lax.psum((self_part, mean_part, bias_part), ('grp', 'blk'))  135 us
    psum x1, blocking collectives, local(): lax.psum((self_part, mean_part, bias_part), ('grp', 'blk'))  116 us
    unnamed x1, blocking collectives  115 us
    scatter-add x1, other arithmetic, edge_total(): jax.ops.segment_sum(usable.astype(jnp.float32), target, buckets + 1)  50.1 us
    all_to_all x1, starting transfers between devices, local(): lax.all_to_all(partials, 'grp', split_axis=0, concat_axis=0, tiled=True)  39 us
    all_gather x1, blocking collectives, local(): hub_back = lax.all_gather(mean_rows[regular:], 'blk', axis=0, tiled=True)  35.6 us
    all_to_all x1, starting transfers between devices, local(): lax.all_to_all(slot_tally, 'grp', split_axis=0, concat_axis=0, tiled=True)  19.2 us
  transfers between devices with their start and end apart: 5, of which 2 were waited for; matrix products, arithmetic and copies ran while one was open for 13% of the time, Pallas kernels for 0%

commit v1 on v0

v1 whole, which is shorter than its diff:
```python
import jax
import jax.numpy as jnp
from jax import lax
from jax.experimental import pallas as pl
from jax.experimental.pallas import tpu as pltpu
from jax.sharding import PartitionSpec as P

MESH = pl.DeviceIdType.MESH
F32 = jnp.float32
BF16 = jnp.bfloat16
FEAT = 128
WIDE = 256
HUBS = 16
LOW = 256
CHUNK = 2048
PIECES = ((4, 3, 5, 2), (6, 1, 7, 0))


def dot_nn(a, b):
    return jnp.dot(a, b, preferred_element_type=F32)


def dot_nt(a, b):
    return lax.dot_general(a, b, (((1,), (1,)), ((), ())), preferred_element_type=F32)


def one_hot(count, row):
    places = lax.broadcasted_iota(jnp.int32, (count, row.shape[1]), 0)
    return (places == row).astype(F32).astype(BF16)


def picks(row, value):
    return (row == value).astype(F32).astype(BF16)


def long_row(ref, start, rows):
    return jnp.concatenate([ref[pl.ds(start + j, 1), :] for j in range(rows)], axis=1)


def await_bytes(ref, sem):
    pltpu.make_async_copy(ref, ref, sem).wait()


def layer_rows(x, mean, upstream, self_weight, mean_weight, bias):
    pre = dot_nn(x, self_weight) + dot_nn(mean, mean_weight) + bias
    sig = jax.nn.sigmoid(pre)
    act = (pre * sig).astype(BF16)
    grad = (upstream.astype(F32) * sig * (1.0 + pre * (1.0 - sig))).astype(BF16)
    return act, grad


def kernel(
    count_ref, feat, cot, w_self, w_mean, bias, src, tgt, rows_in,
    act, fgrad, self_grad, mean_grad, bias_grad,
    ohs, oht, gath, high, xt4, rl, cnt, acc, sums, nmean, pgrad, mrt4, own,
    out_slots, in_slots, back_out, back_in,
    tal_out, tal_in, cnt_out, cnt_in, hub_out, hub_in, hubs_out, hubs_in,
    w1_out, w1_in, b1_out, b1_in, w2_out, w2_in, b2_out, b2_in, w3_out, w3_in, small,
    send_sem, recv_sem, slot_sem, back_sem,
):
    grp = lax.axis_index("grp")
    blk = lax.axis_index("blk")
    chip = lax.div(grp, 2)
    core = lax.rem(grp, 2)
    sibling = grp + 1 - 2 * core
    n_grp, n_blk = 16, 64
    blocks = tgt.shape[0]
    per = CHUNK // 128
    chunks = blocks // per

    barrier = pltpu.get_barrier_semaphore()

    def greet(axis, me, n):
        def body(i, carry):
            pl.semaphore_signal(
                barrier, inc=1, device_id={axis: lax.rem(me + i, n)}, device_id_type=MESH
            )
            return carry

        lax.fori_loop(1, n, body, 0)

    greet("blk", blk, n_blk)
    greet("grp", grp, n_grp)

    def send(axis, peer, source, target, which, arrive):
        pltpu.make_async_remote_copy(
            src_ref=source, dst_ref=target, send_sem=send_sem.at[which], recv_sem=arrive,
            device_id={axis: peer}, device_id_type=MESH,
        ).start()

    def send_all(axis, source, target, which):
        me, n = (blk, n_blk) if axis == "blk" else (grp, n_grp)

        def body(i, carry):
            peer = lax.rem(me + i, n)
            send(axis, peer, source(peer), target.at[me], which, recv_sem.at[which])
            return carry

        lax.fori_loop(1, n, body, 0)

    def arrived(target, which):
        n = target.shape[0]
        await_bytes(target.at[pl.ds(0, n - 1)], recv_sem.at[which])

    eye_small = (
        lax.broadcasted_iota(jnp.int32, (FEAT, FEAT), 0)
        == lax.broadcasted_iota(jnp.int32, (FEAT, FEAT), 1)
    ).astype(F32).astype(BF16)
    eye_low = (
        lax.broadcasted_iota(jnp.int32, (LOW, LOW), 0)
        == lax.broadcasted_iota(jnp.int32, (LOW, LOW), 1)
    ).astype(F32).astype(BF16)

    live = lax.broadcasted_iota(jnp.int32, (blocks, 128), 0) < count_ref[0, 0]
    high[...] = jnp.where(live, lax.shift_right_logical(tgt[...], 8), 99)
    for s in range(4):
        xt4[s * FEAT:(s + 1) * FEAT, :] = dot_nt(
            eye_small, feat[s * LOW:(s + 1) * LOW, :]
        ).astype(BF16)

    cnt[...] = jnp.zeros_like(cnt)

    def take_sources(c, carry):
        source = long_row(src, c * per, per)
        ohs[c] = one_hot(LOW, source & 255)
        oht[c] = one_hot(LOW, long_row(tgt, c * per, per) & 255)
        part = lax.shift_right_logical(source, 8)
        total = jnp.zeros((FEAT, CHUNK), F32)
        for s in range(4):
            total = jnp.where(
                part == s, dot_nn(xt4[s * FEAT:(s + 1) * FEAT, :], ohs[c]), total
            )
        gath[c] = total.astype(BF16)
        cnt[...] += dot_nt(one_hot(16, long_row(high, c * per, per)), oht[c])
        return carry

    lax.fori_loop(0, chunks, take_sources, 0)

    for p in range(n_grp):
        tal_out[p] = (
            cnt[p // 2:p // 2 + 1, (p % 2) * 128:(p % 2) * 128 + 128].astype(BF16).astype(F32)
        )
    cnt_out[...] = jnp.concatenate(
        [cnt[8 + r // 2:9 + r // 2, (r % 2) * 128:(r % 2) * 128 + 128] for r in range(8)], axis=0
    )
    pl.semaphore_wait(barrier, n_blk + n_grp - 2)
    send_all("grp", lambda peer: tal_out.at[peer], tal_in, 0)
    send_all("blk", lambda peer: cnt_out, cnt_in, 1)
    tal_in[grp] = tal_out[grp]
    cnt_in[blk] = cnt_out[...]

    def add_targets(parts):
        acc[...] = jnp.zeros_like(acc)

        def body(c, carry):
            row = long_row(high, c * per, per)
            gathered = gath[c]
            acc[...] += dot_nt(
                jnp.concatenate([gathered * picks(row, t) for t in parts], axis=0), oht[c]
            )
            return carry

        lax.fori_loop(0, chunks, body, 0)

    def slot_piece(offsets):
        towards = [lax.rem(chip + d, 8) for d in offsets]
        add_targets(towards)
        for k, (d, z) in enumerate(zip(offsets, towards)):
            for j in range(2):
                out_slots[2 * z + j] = acc[
                    k * FEAT:(k + 1) * FEAT, j * 128:(j + 1) * 128
                ].astype(BF16)
            for j in range(2):
                if d:
                    peer = 2 * z + j
                elif j:
                    continue
                else:
                    peer = sibling
                send("grp", peer, out_slots.at[peer], in_slots.at[grp], 2, slot_sem.at[d])

    slot_piece(PIECES[0])
    add_targets(range(8, 12))
    for t in range(4):
        turned = dot_nt(eye_low, acc[t * FEAT:(t + 1) * FEAT, :].astype(BF16)).astype(BF16)
        hub_out[t * 16:(t + 1) * 16] = turned.reshape(16, HUBS, FEAT)
    send_all("blk", lambda peer: hub_out.at[peer], hub_in, 3)
    hub_in[blk] = hub_out[blk]
    slot_piece(PIECES[1])
    in_slots[grp] = out_slots[grp]

    for z in range(8):
        rl[z] = one_hot(LOW, long_row(rows_in, 2 * z, 2) & 255)
    arrived(tal_in, 0)
    degree_column = jnp.zeros((LOW, 16), F32)
    degree_row = jnp.zeros((16, LOW), F32)
    for z in range(8):
        place = lax.shift_right_logical(long_row(rows_in, 2 * z, 2), 8)
        tally = jnp.concatenate([tal_in[2 * z], tal_in[2 * z + 1]], axis=1)
        kinds = lax.broadcasted_iota(jnp.int32, (16, LOW), 0)
        marked = jnp.where(kinds == place, tally, 0.0).astype(BF16)
        degree_column += dot_nt(rl[z], marked)
        degree_row += dot_nt(marked, rl[z])
    over_column = 1.0 / jnp.maximum(degree_column, 1.0)
    over_row = 1.0 / jnp.maximum(degree_row, 1.0)

    def from_offset(buffer, sems, d):
        z = lax.rem(chip + 8 - d, 8)
        if d:
            await_bytes(buffer.at[pl.ds(2 * z, 2)], sems.at[d])
        else:
            await_bytes(buffer.at[sibling], sems.at[d])
        return z

    order = PIECES[0] + PIECES[1]
    sums[...] = jnp.zeros_like(sums)
    for d in order:
        z = from_offset(in_slots, slot_sem, d)
        place = lax.shift_right_logical(long_row(rows_in, 2 * z, 2), 8)
        block = jnp.concatenate([in_slots[2 * z], in_slots[2 * z + 1]], axis=1)
        spread = jnp.concatenate([block * picks(place, h) for h in range(4)], axis=0)
        sums[...] += dot_nt(rl[z], spread)

    for h in range(4):
        here = slice(h * LOW, (h + 1) * LOW)
        mean = (sums[:, h * FEAT:(h + 1) * FEAT] * over_column[:, h:h + 1]).astype(BF16)
        nmean[here, :] = mean
        a, g = layer_rows(feat[here, :], mean, cot[here, :], w_self[...], w_mean[...], bias[...])
        act[here, :] = a
        pgrad[here, :] = g
        mrt4[h * FEAT:(h + 1) * FEAT, :] = (
            dot_nt(w_mean[...], g) * over_row[h:h + 1, :]
        ).astype(BF16)

    for d in order:
        z = lax.rem(chip + d, 8)
        place = lax.shift_right_logical(long_row(rows_in, 2 * z, 2), 8)
        every = dot_nn(mrt4[...], rl[z])
        taken = every[:FEAT]
        for h in range(1, 4):
            taken = jnp.where(place == h, every[h * FEAT:(h + 1) * FEAT], taken)
        taken = taken.astype(BF16)
        for j in range(2):
            back_out[2 * z + j] = taken[:, j * 128:(j + 1) * 128]
        for j in range(2):
            if d:
                peer = 2 * z + j
            elif j:
                continue
            else:
                peer = sibling
            send("grp", peer, back_out.at[peer], back_in.at[grp], 4, back_sem.at[d])
    back_in[grp] = back_out[grp]

    first = 4 * LOW - HUBS
    arrived(cnt_in, 1)
    small[...] = jnp.sum(cnt_in[...], axis=0)
    hub_counts = small[pl.ds(lax.div(blk, 8), 1), :]
    lanes = lax.broadcasted_iota(jnp.int32, (HUBS, 128), 1)
    mine = lanes == lax.broadcasted_iota(jnp.int32, (HUBS, 128), 0) + lax.rem(blk, 8) * HUBS
    hub_degree = jnp.sum(jnp.where(mine, hub_counts, 0.0), axis=1, keepdims=True)
    over_hub = 1.0 / jnp.maximum(hub_degree, 1.0)
    arrived(hub_in, 3)
    hub_mean = (jnp.sum(hub_in[...].astype(F32), axis=0) * over_hub).astype(BF16)
    nmean[first:, :] = hub_mean
    a, g = layer_rows(
        feat[first:, :], hub_mean, cot[first:, :], w_self[...], w_mean[...], bias[...]
    )
    act[first:, :] = a
    pgrad[first:, :] = g
    hubs_out[...] = (dot_nt(g, w_mean[...]) * over_hub).astype(BF16)
    send_all("blk", lambda peer: hubs_out, hubs_in, 5)
    hubs_in[blk] = hubs_out[...]

    self_part = jnp.zeros((FEAT, WIDE), F32)
    mean_part = jnp.zeros((FEAT, WIDE), F32)
    bias_part = jnp.zeros((1, WIDE), F32)
    for h in range(4):
        here = slice(h * LOW, (h + 1) * LOW)
        g = pgrad[here, :]
        self_part += dot_nn(xt4[h * FEAT:(h + 1) * FEAT, :], g)
        mean_part += dot_nn(dot_nt(eye_small, nmean[here, :]).astype(BF16), g)
        bias_part += jnp.sum(g.astype(F32), axis=0, keepdims=True)
    for k, part in enumerate((self_part, mean_part)):
        for j in range(2):
            w1_out[(2 * k + j) * 16:(2 * k + j + 1) * 16] = (
                part[:, j * 128:(j + 1) * 128].reshape(16, 8, 128)
            )
    b1_out[...] = bias_part
    send_all("blk", lambda peer: w1_out.at[peer], w1_in, 6)
    send_all("blk", lambda peer: b1_out, b1_in, 7)
    w1_in[blk] = w1_out[blk]
    b1_in[blk] = b1_out[...]

    for h in range(4):
        here = slice(h * LOW, (h + 1) * LOW)
        own[here, :] = dot_nt(pgrad[here, :], w_self[...])

    arrived(w1_in, 6)
    arrived(b1_in, 7)
    w2_out[...] = jnp.sum(w1_in[...], axis=0)
    b2_out[...] = jnp.sum(b1_in[...], axis=0)
    send_all("grp", lambda peer: w2_out, w2_in, 8)
    send_all("grp", lambda peer: b2_out, b2_in, 9)
    w2_in[grp] = w2_out[...]
    b2_in[grp] = b2_out[...]

    def take_targets(table, part, fresh):
        def body(c, carry):
            row = long_row(high, c * per, per)
            before = jnp.zeros((FEAT, CHUNK), F32) if fresh else gath[c].astype(F32)
            for t, block in zip(part, table):
                before = jnp.where(row == t, dot_nn(block, oht[c]), before)
            gath[c] = before.astype(BF16)
            return carry

        lax.fori_loop(0, chunks, body, 0)

    arrived(hubs_in, 5)
    take_targets(
        [
            dot_nt(eye_small, hubs_in[t * 16:(t + 1) * 16].reshape(LOW, FEAT)).astype(BF16)
            for t in range(4)
        ],
        range(8, 12),
        True,
    )

    def back_piece(offsets):
        places = [from_offset(back_in, back_sem, d) for d in offsets]
        take_targets(
            [jnp.concatenate([back_in[2 * z], back_in[2 * z + 1]], axis=1) for z in places],
            places,
            False,
        )

    back_piece(order[:4])
    arrived(w2_in, 8)
    arrived(b2_in, 9)
    w3_out[...] = jnp.sum(w2_in[...], axis=0)
    bias_grad[...] = jnp.sum(b2_in[...], axis=0)
    send_all("blk", lambda peer: w3_out, w3_in, 10)
    w3_in[blk] = w3_out[...]
    back_piece(order[4:])

    sums[...] = jnp.zeros_like(sums)

    def add_sources(c, carry):
        part = lax.shift_right_logical(long_row(src, c * per, per), 8)
        gathered = gath[c]
        sums[...] += dot_nt(
            ohs[c], jnp.concatenate([gathered * picks(part, s) for s in range(4)], axis=0)
        )
        return carry

    lax.fori_loop(0, chunks, add_sources, 0)
    for s in range(4):
        here = slice(s * LOW, (s + 1) * LOW)
        fgrad[here, :] = (own[here, :] + sums[:, s * FEAT:(s + 1) * FEAT]).astype(BF16)

    arrived(w3_in, 10)
    for k, grad in enumerate((self_grad, mean_grad)):
        for j in range(2):
            grad[:, j * 128:(j + 1) * 128] = (
                w3_in[(2 * k + j) * 16:(2 * k + j + 1) * 16].reshape(FEAT, 128)
            )

    sent = ((tal_in, 0), (cnt_in, 1), (in_slots, 2), (hub_in, 3), (back_in, 4), (hubs_in, 5),
            (w1_in, 6), (b1_in, 7), (w2_in, 8), (b2_in, 9), (w3_in, 10))
    for buffer, which in sent:
        await_bytes(buffer.at[pl.ds(0, buffer.shape[0] - 1)], send_sem.at[which])


def local(
    features, cotangent, self_weight, mean_weight, bias_term,
    edge_source, edge_target, block_counts, receive_rows,
):
    vertices = features.shape[0]
    blocks = edge_source.shape[2]
    chunks = blocks * 128 // CHUNK
    whole = pl.BlockSpec(memory_space=pltpu.VMEM)
    shape = jax.ShapeDtypeStruct
    act, fgrad, self_grad, mean_grad, bias_grad = pl.pallas_call(
        kernel,
        out_shape=(
            shape((vertices, WIDE), BF16),
            shape((vertices, FEAT), BF16),
            shape((FEAT, WIDE), F32),
            shape((FEAT, WIDE), F32),
            shape((1, WIDE), F32),
        ),
        in_specs=[pl.BlockSpec(memory_space=pltpu.SMEM)] + [whole] * 8,
        out_specs=[whole] * 5,
        scratch_shapes=[
            pltpu.VMEM((chunks, LOW, CHUNK), BF16),
            pltpu.VMEM((chunks, LOW, CHUNK), BF16),
            pltpu.VMEM((chunks, FEAT, CHUNK), BF16),
            pltpu.VMEM((blocks, 128), jnp.int32),
            pltpu.VMEM((4 * FEAT, LOW), BF16),
            pltpu.VMEM((8, LOW, 256), BF16),
            pltpu.VMEM((16, LOW), F32),
            pltpu.VMEM((4 * FEAT, LOW), F32),
            pltpu.VMEM((LOW, 4 * FEAT), F32),
            pltpu.VMEM((vertices, FEAT), BF16),
            pltpu.VMEM((vertices, WIDE), BF16),
            pltpu.VMEM((4 * FEAT, LOW), BF16),
            pltpu.VMEM((vertices, FEAT), F32),
            pltpu.VMEM((16, FEAT, 128), BF16),
            pltpu.VMEM((16, FEAT, 128), BF16),
            pltpu.VMEM((16, FEAT, 128), BF16),
            pltpu.VMEM((16, FEAT, 128), BF16),
            pltpu.VMEM((16, 1, 128), F32),
            pltpu.VMEM((16, 1, 128), F32),
            pltpu.VMEM((8, 128), F32),
            pltpu.VMEM((64, 8, 128), F32),
            pltpu.VMEM((64, HUBS, FEAT), BF16),
            pltpu.VMEM((64, HUBS, FEAT), BF16),
            pltpu.VMEM((HUBS, FEAT), BF16),
            pltpu.VMEM((64, HUBS, FEAT), BF16),
            pltpu.VMEM((64, 8, 128), F32),
            pltpu.VMEM((64, 8, 128), F32),
            pltpu.VMEM((1, WIDE), F32),
            pltpu.VMEM((64, 1, WIDE), F32),
            pltpu.VMEM((8, 128), F32),
            pltpu.VMEM((16, 8, 128), F32),
            pltpu.VMEM((1, WIDE), F32),
            pltpu.VMEM((16, 1, WIDE), F32),
            pltpu.VMEM((8, 128), F32),
            pltpu.VMEM((64, 8, 128), F32),
            pltpu.VMEM((8, 128), F32),
            pltpu.SemaphoreType.DMA((11,)),
            pltpu.SemaphoreType.DMA((11,)),
            pltpu.SemaphoreType.DMA((8,)),
            pltpu.SemaphoreType.DMA((8,)),
        ],
        compiler_params=pltpu.CompilerParams(
            collective_id=0, has_side_effects=True, vmem_limit_bytes=50 * 1024 * 1024
        ),
        name="sage_layer",
    )(
        block_counts,
        features,
        cotangent,
        self_weight,
        mean_weight,
        bias_term.reshape(1, WIDE),
        edge_source.reshape(blocks, 128),
        edge_target.reshape(blocks, 128),
        receive_rows.reshape(16, 128),
    )
    return act, fgrad, self_grad, mean_grad, bias_grad.reshape(WIDE)


def solution(mesh):
    placed = (
        P(("grp", "blk"), None),
        P(("grp", "blk"), None),
        P(),
        P(),
        P(),
        P("grp", "blk", None, None),
        P("grp", "blk", None, None),
        P("grp", "blk"),
        P("grp", "blk", None, None),
    )
    return jax.shard_map(
        local,
        mesh=mesh,
        in_specs=placed,
        out_specs=(P(("grp", "blk"), None), P(("grp", "blk"), None), P(), P(), P()),
        check_vma=False,
    )
```

time: 736 us -> 91.8 us (0.12)
  blocking collectives: 267 us -> 0 us
  other arithmetic: 228 us -> 0 us
  waiting for transfers between devices: 137 us -> 0 us
  Pallas kernels: 0 us -> 80.1 us
  starting transfers between devices: 64.3 us -> 0 us
  between operations: 15.6 us -> 1.33 us
    scatter-add x5 -> x0, other arithmetic: 227 us -> none  [the longest x2 151 us: edge_total(): jax.ops.segment_sum(source_table[take_index.reshape(-1)].astype(jnp.float...]
    psum x1 -> x0, waiting for transfers between devices: 135 us -> none  [local(): lax.psum((self_part, mean_part, bias_part), ('grp', 'blk'))]
    psum x1 -> x0, blocking collectives: 116 us -> none  [local(): lax.psum((self_part, mean_part, bias_part), ('grp', 'blk'))]
    unnamed x1 -> x0, blocking collectives: 115 us -> none
    pallas_call x0 -> x1, Pallas kernels: none -> 80.1 us  [local(): pl.pallas_call(kernel, out_shape=(shape((vertices, WIDE), BF16), shape((v...]
    all_to_all x3 -> x0, starting transfers between devices: 64.3 us -> none  [the longest x1 39 us: local(): lax.all_to_all(partials, 'grp', split_axis=0, concat_axis=0, tiled=True)]
    all_gather x1 -> x0, blocking collectives: 35.6 us -> none  [local(): hub_back = lax.all_gather(mean_rows[regular:], 'blk', axis=0, tiled=True)]
    gather x1 -> x0, local copies, waits for them, and re-layouts: 7.97 us -> none  [local(): mean_rows[row_index].reshape(groups, capacity, feature_width)]
  transfers between devices with their start and end apart: 5 -> 0, of which waited for: 2 -> 0; matrix products, arithmetic and copies ran while one was open for 13% -> 0% of each run, Pallas kernels for 0% -> 0%
where the time goes in v1:
time: 91.8 us; the launch traced here: 90.7 us
  Pallas kernels  80.1 us (87%)
  local copies, waits for them, and re-layouts  9.23 us (10%)
  between operations  1.33 us (1%)
    pallas_call x1, Pallas kernels, local(): pl.pallas_call(kernel, out_shape=(shape((vertices, WIDE), BF16), shape((v...  80.1 us
    unnamed x21, local copies, waits for them, and re-layouts  9.23 us

profile of v1, /device:TPU:1, one launch (start us, length us, event | category | flops | bytes accessed | tf_op | source)
XLA Modules:
  0.0 90.7 jit_solution(4463745545489235086)
XLA Ops:
  0.6 0.0 copy-start.6
  1.3 0.0 copy-start.7
  1.3 0.0 copy-done.6
  1.3 0.7 copy-done.7
  2.0 0.0 copy-start
  2.0 1.0 %copy-done = bf16[1024,256]{1,0:T(8,128)(2,1)S(1)} copy-done((bf16[1024,256]{1,0:T(8,128)(2,1)S(1)}, bf16[1024,256]{1,0:T(8,128)(2,1)}, u32[]{:S(2)}) %copy-start) | copy-done | bytes 524312
  3.0 0.0 copy-start.1
  3.0 0.9 %copy-done.1 = bf16[1024,128]{1,0:T(8,128)(2,1)S(1)} copy-done((bf16[1024,128]{1,0:T(8,128)(2,1)S(1)}, bf16[1024,128]{1,0:T(8,128)(2,1)}, u32[]{:S(2)}) %copy-start.1) | copy-done | bytes 262168
  4.0 0.0 copy-start.2
  4.0 0.8 copy-done.2
  4.8 0.0 copy-start.3
  4.8 0.8 copy-done.3
  5.7 0.0 copy-start.4
  5.7 0.8 copy-done.4
  6.4 0.0 copy-start.5
  6.4 0.8 copy-done.5
  7.2 80.1 %sage_layer.1 = (bf16[1024,256]{1,0:T(8,128)(2,1)S(1)}, bf16[1024,128]{1,0:T(8,128)(2,1)S(1)}, f32[128,256]{1,0:T(8,128)S(1)}, f32[128,256]{1,0:T(8,128)S(1)}, f32[1,256]{1,0:T(1,128)S(1)}) custom-call(s32[1,1]{1,0:T(1,128)S(6)} %copy.19.count_ref, bf16[1024,128]{1,0:T(8,128)(2,1)S(1)} %copy-done.1, bf16[1024,256]{1,0:T(8,128)(2,1)S(1)} %copy-done, ...), custom_call_target="tpu_custom_call" | custom-call | tf_op jit(solution)/shard_map/sage_layer/pallas_call | solution.py:383
  87.3 0.8 copy.20
  88.1 0.7 copy.21
  88.8 0.7 copy.22
  89.5 0.7 copy.23
  90.1 0.6 copy.24
Async XLA Ops:
  0.6 0.7 copy-start.6
  1.3 0.7 copy-start.7
  2.0 1.0 %copy-start = (bf16[1024,256]{1,0:T(8,128)(2,1)S(1)}, bf16[1024,256]{1,0:T(8,128)(2,1)}, u32[]{:S(2)}) copy-start(bf16[1024,256]{1,0:T(8,128)(2,1)} %cot.1) | copy-start | bytes 1572868
  3.0 0.9 %copy-start.1 = (bf16[1024,128]{1,0:T(8,128)(2,1)S(1)}, bf16[1024,128]{1,0:T(8,128)(2,1)}, u32[]{:S(2)}) copy-start(bf16[1024,128]{1,0:T(8,128)(2,1)} %feat.1) | copy-start | bytes 786436
  4.0 0.8 copy-start.2
  4.8 0.8 copy-start.3
  5.7 0.8 copy-start.4
  6.4 0.8 copy-start.5

commit v2 on v1

--- a/solution.py
+++ b/solution.py
@@ -50,14 +50,24 @@
 
 
 def kernel(
-    count_ref, feat, cot, w_self, w_mean, bias, src, tgt, rows_in,
-    act, fgrad, self_grad, mean_grad, bias_grad,
+    count_ref, feat_hbm, cot_hbm, w_self_hbm, w_mean_hbm, bias_hbm, src_hbm, tgt_hbm, rows_hbm,
+    act_hbm, fgrad_hbm, self_grad, mean_grad, bias_grad,
+    feat, cot, w_self, w_mean, bias, src, tgt, rows_in, act, fgrad,
     ohs, oht, gath, high, xt4, rl, cnt, acc, sums, nmean, pgrad, mrt4, own,
     out_slots, in_slots, back_out, back_in,
     tal_out, tal_in, cnt_out, cnt_in, hub_out, hub_in, hubs_out, hubs_in,
-    w1_out, w1_in, b1_out, b1_in, w2_out, w2_in, b2_out, b2_in, w3_out, w3_in, small,
-    send_sem, recv_sem, slot_sem, back_sem,
+    w1_out, w1_in, b1_out, b1_in, w2_out, w2_in, b2_out, b2_in, w3_out, w3_in, small, relay_in,
+    send_sem, recv_sem, slot_sem, back_sem, relay_sem, load_sem, store_sem,
 ):
+    loads = [
+        pltpu.make_async_copy(source, target, load_sem.at[k])
+        for k, (source, target) in enumerate((
+            (tgt_hbm, tgt), (src_hbm, src), (feat_hbm, feat), (rows_hbm, rows_in),
+            (w_mean_hbm, w_mean), (w_self_hbm, w_self), (bias_hbm, bias), (cot_hbm, cot),
+        ))
+    ]
+    for copy in loads:
+        copy.start()
     grp = lax.axis_index("grp")
     blk = lax.axis_index("blk")
     chip = lax.div(grp, 2)
@@ -110,6 +120,9 @@
         lax.broadcasted_iota(jnp.int32, (LOW, LOW), 0)
         == lax.broadcasted_iota(jnp.int32, (LOW, LOW), 1)
     ).astype(F32).astype(BF16)
+
+    for copy in loads[:3]:
+        copy.wait()
 
     live = lax.broadcasted_iota(jnp.int32, (blocks, 128), 0) < count_ref[0, 0]
     high[...] = jnp.where(live, lax.shift_right_logical(tgt[...], 8), 99)
@@ -150,17 +163,44 @@
     cnt_in[blk] = cnt_out[...]
 
     def add_targets(parts):
-        acc[...] = jnp.zeros_like(acc)
+        size = len(parts) * FEAT
+        acc[:size, :] = jnp.zeros((size, LOW), F32)
 
         def body(c, carry):
             row = long_row(high, c * per, per)
             gathered = gath[c]
-            acc[...] += dot_nt(
+            acc[:size, :] += dot_nt(
                 jnp.concatenate([gathered * picks(row, t) for t in parts], axis=0), oht[c]
             )
             return carry
 
         lax.fori_loop(0, chunks, body, 0)
+
+    before, across = lax.rem(chip + 7, 8), lax.rem(chip + 5, 8)
+    after = lax.rem(chip + 1, 8)
+
+    def send_blocks(d, z, out, into, which, sems):
+        if d == 0:
+            send("grp", sibling, out.at[sibling], into.at[grp], which, sems.at[d])
+        elif d == 4:
+            straight = 2 * z + core
+            send("grp", straight, out.at[straight], into.at[grp], which, sems.at[d])
+            relay = relay_in.at[which // 4]
+            send(
+                "grp", 2 * before + core, out.at[2 * z + 1 - core], relay,
+                which, relay_sem.at[which // 4],
+            )
+        else:
+            for j in range(2):
+                send("grp", 2 * z + j, out.at[2 * z + j], into.at[grp], which, sems.at[d])
+
+    def hand_over(into, which, sems):
+        relay = relay_in.at[which // 4]
+        await_bytes(relay, relay_sem.at[which // 4])
+        send(
+            "grp", 2 * across + 1 - core, relay, into.at[2 * after + core],
+            11 + which // 4, sems.at[4],
+        )
 
     def slot_piece(offsets):
         towards = [lax.rem(chip + d, 8) for d in offsets]
@@ -170,14 +210,7 @@
                 out_slots[2 * z + j] = acc[
                     k * FEAT:(k + 1) * FEAT, j * 128:(j + 1) * 128
                 ].astype(BF16)
-            for j in range(2):
-                if d:
-                    peer = 2 * z + j
-                elif j:
-                    continue
-                else:
-                    peer = sibling
-                send("grp", peer, out_slots.at[peer], in_slots.at[grp], 2, slot_sem.at[d])
+            send_blocks(d, z, out_slots, in_slots, 2, slot_sem)
 
     slot_piece(PIECES[0])
     add_targets(range(8, 12))
@@ -186,8 +219,12 @@
         hub_out[t * 16:(t + 1) * 16] = turned.reshape(16, HUBS, FEAT)
     send_all("blk", lambda peer: hub_out.at[peer], hub_in, 3)
     hub_in[blk] = hub_out[blk]
+    hand_over(in_slots, 2, slot_sem)
     slot_piece(PIECES[1])
     in_slots[grp] = out_slots[grp]
+
+    for copy in loads[3:]:
+        copy.wait()
 
     for z in range(8):
         rl[z] = one_hot(LOW, long_row(rows_in, 2 * z, 2) & 255)
@@ -214,7 +251,7 @@
 
     order = PIECES[0] + PIECES[1]
     sums[...] = jnp.zeros_like(sums)
-    for d in order:
+    for d in order[1:] + order[:1]:
         z = from_offset(in_slots, slot_sem, d)
         place = lax.shift_right_logical(long_row(rows_in, 2 * z, 2), 8)
         block = jnp.concatenate([in_slots[2 * z], in_slots[2 * z + 1]], axis=1)
@@ -242,14 +279,7 @@
         taken = taken.astype(BF16)
         for j in range(2):
             back_out[2 * z + j] = taken[:, j * 128:(j + 1) * 128]
-        for j in range(2):
-            if d:
-                peer = 2 * z + j
-            elif j:
-                continue
-            else:
-                peer = sibling
-            send("grp", peer, back_out.at[peer], back_in.at[grp], 4, back_sem.at[d])
+        send_blocks(d, z, back_out, back_in, 4, back_sem)
     back_in[grp] = back_out[grp]
 
     first = 4 * LOW - HUBS
@@ -263,14 +293,13 @@
     arrived(hub_in, 3)
     hub_mean = (jnp.sum(hub_in[...].astype(F32), axis=0) * over_hub).astype(BF16)
     nmean[first:, :] = hub_mean
-    a, g = layer_rows(
+    a, hub_grad = layer_rows(
         feat[first:, :], hub_mean, cot[first:, :], w_self[...], w_mean[...], bias[...]
     )
     act[first:, :] = a
-    pgrad[first:, :] = g
-    hubs_out[...] = (dot_nt(g, w_mean[...]) * over_hub).astype(BF16)
-    send_all("blk", lambda peer: hubs_out, hubs_in, 5)
-    hubs_in[blk] = hubs_out[...]
+    pgrad[first:, :] = hub_grad
+    act_copy = pltpu.make_async_copy(act, act_hbm, store_sem.at[0])
+    act_copy.start()
 
     self_part = jnp.zeros((FEAT, WIDE), F32)
     mean_part = jnp.zeros((FEAT, WIDE), F32)
@@ -292,6 +321,10 @@
     w1_in[blk] = w1_out[blk]
     b1_in[blk] = b1_out[...]
 
+    hubs_out[...] = (dot_nt(hub_grad, w_mean[...]) * over_hub).astype(BF16)
+    send_all("blk", lambda peer: hubs_out, hubs_in, 5)
+    hubs_in[blk] = hubs_out[...]
+    hand_over(back_in, 4, back_sem)
     for h in range(4):
         here = slice(h * LOW, (h + 1) * LOW)
         own[here, :] = dot_nt(pgrad[here, :], w_self[...])
@@ -305,59 +338,51 @@
     w2_in[grp] = w2_out[...]
     b2_in[grp] = b2_out[...]
 
-    def take_targets(table, part, fresh):
+    sums[...] = jnp.zeros_like(sums)
+
+    def take_targets(table, part, first_piece):
         def body(c, carry):
             row = long_row(high, c * per, per)
-            before = jnp.zeros((FEAT, CHUNK), F32) if fresh else gath[c].astype(F32)
+            before = jnp.zeros((FEAT, CHUNK), F32) if first_piece else gath[c].astype(F32)
             for t, block in zip(part, table):
                 before = jnp.where(row == t, dot_nn(block, oht[c]), before)
-            gath[c] = before.astype(BF16)
+            gathered = before.astype(BF16)
+            if first_piece:
+                gath[c] = gathered
+                return carry
+            kind = lax.shift_right_logical(long_row(src, c * per, per), 8)
+            sums[...] += dot_nt(
+                ohs[c], jnp.concatenate([gathered * picks(kind, s) for s in range(4)], axis=0)
+            )
             return carry
 
         lax.fori_loop(0, chunks, body, 0)
 
-    arrived(hubs_in, 5)
-    take_targets(
-        [
-            dot_nt(eye_small, hubs_in[t * 16:(t + 1) * 16].reshape(LOW, FEAT)).astype(BF16)
-            for t in range(4)
-        ],
-        range(8, 12),
-        True,
-    )
-
-    def back_piece(offsets):
+    def back_table(offsets):
         places = [from_offset(back_in, back_sem, d) for d in offsets]
-        take_targets(
-            [jnp.concatenate([back_in[2 * z], back_in[2 * z + 1]], axis=1) for z in places],
-            places,
-            False,
-        )
-
-    back_piece(order[:4])
+        table = [jnp.concatenate([back_in[2 * z], back_in[2 * z + 1]], axis=1) for z in places]
+        return table, places
+
+    take_targets(*back_table(order[1:5]), True)
     arrived(w2_in, 8)
     arrived(b2_in, 9)
     w3_out[...] = jnp.sum(w2_in[...], axis=0)
     bias_grad[...] = jnp.sum(b2_in[...], axis=0)
     send_all("blk", lambda peer: w3_out, w3_in, 10)
     w3_in[blk] = w3_out[...]
-    back_piece(order[4:])
-
-    sums[...] = jnp.zeros_like(sums)
-
-    def add_sources(c, carry):
-        part = lax.shift_right_logical(long_row(src, c * per, per), 8)
-        gathered = gath[c]
-        sums[...] += dot_nt(
-            ohs[c], jnp.concatenate([gathered * picks(part, s) for s in range(4)], axis=0)
-        )
-        return carry
-
-    lax.fori_loop(0, chunks, add_sources, 0)
+    table, places = back_table(order[5:] + order[:1])
+    arrived(hubs_in, 5)
+    table += [
+        dot_nt(eye_small, hubs_in[t * 16:(t + 1) * 16].reshape(LOW, FEAT)).astype(BF16)
+        for t in range(4)
+    ]
+    take_targets(table, places + [8, 9, 10, 11], False)
     for s in range(4):
         here = slice(s * LOW, (s + 1) * LOW)
         fgrad[here, :] = (own[here, :] + sums[:, s * FEAT:(s + 1) * FEAT]).astype(BF16)
 
+    fgrad_copy = pltpu.make_async_copy(fgrad, fgrad_hbm, store_sem.at[1])
+    fgrad_copy.start()
     arrived(w3_in, 10)
     for k, grad in enumerate((self_grad, mean_grad)):
         for j in range(2):
@@ -369,6 +394,24 @@
             (w1_in, 6), (b1_in, 7), (w2_in, 8), (b2_in, 9), (w3_in, 10))
     for buffer, which in sent:
         await_bytes(buffer.at[pl.ds(0, buffer.shape[0] - 1)], send_sem.at[which])
+    for k in range(2):
+        await_bytes(relay_in.at[k], send_sem.at[11 + k])
+    act_copy.wait()
+    fgrad_copy.wait()
+
+
+def hand_on(*refs):
+    n = 5
+    given, wanted, held, came, left = refs[:n], refs[n:2 * n], refs[2 * n:3 * n], refs[-2], refs[-1]
+    loads = [pltpu.make_async_copy(given[k], held[k], came.at[k]) for k in range(n)]
+    stores = [pltpu.make_async_copy(held[k], wanted[k], left.at[k]) for k in range(n)]
+    for copy in loads:
+        copy.start()
+    for load, store in zip(loads, stores):
+        load.wait()
+        store.start()
+    for copy in stores:
+        copy.wait()
 
 
 def local(
@@ -380,18 +423,30 @@
     chunks = blocks * 128 // CHUNK
     whole = pl.BlockSpec(memory_space=pltpu.VMEM)
     shape = jax.ShapeDtypeStruct
-    act, fgrad, self_grad, mean_grad, bias_grad = pl.pallas_call(
+    far = pl.BlockSpec(memory_space=pl.ANY)
+    out_shape = (
+        shape((vertices, WIDE), BF16),
+        shape((vertices, FEAT), BF16),
+        shape((FEAT, WIDE), F32),
+        shape((FEAT, WIDE), F32),
+        shape((1, WIDE), F32),
+    )
+    results = pl.pallas_call(
         kernel,
-        out_shape=(
-            shape((vertices, WIDE), BF16),
-            shape((vertices, FEAT), BF16),
-            shape((FEAT, WIDE), F32),
-            shape((FEAT, WIDE), F32),
-            shape((1, WIDE), F32),
-        ),
-        in_specs=[pl.BlockSpec(memory_space=pltpu.SMEM)] + [whole] * 8,
-        out_specs=[whole] * 5,
+        out_shape=out_shape,
+        in_specs=[pl.BlockSpec(memory_space=pltpu.SMEM)] + [pl.BlockSpec(memory_space=pltpu.HBM)] * 8,
+        out_specs=[far] * 2 + [whole] * 3,
         scratch_shapes=[
+            pltpu.VMEM((vertices, FEAT), BF16),
+            pltpu.VMEM((vertices, WIDE), BF16),
+            pltpu.VMEM((FEAT, WIDE), BF16),
+            pltpu.VMEM((FEAT, WIDE), BF16),
+            pltpu.VMEM((1, WIDE), F32),
+            pltpu.VMEM((blocks, 128), jnp.int32),
+            pltpu.VMEM((blocks, 128), jnp.int32),
+            pltpu.VMEM((16, 128), jnp.int32),
+            pltpu.VMEM((vertices, WIDE), BF16),
+            pltpu.VMEM((vertices, FEAT), BF16),
             pltpu.VMEM((chunks, LOW, CHUNK), BF16),
             pltpu.VMEM((chunks, LOW, CHUNK), BF16),
             pltpu.VMEM((chunks, FEAT, CHUNK), BF16),
@@ -428,13 +483,17 @@
             pltpu.VMEM((8, 128), F32),
             pltpu.VMEM((64, 8, 128), F32),
             pltpu.VMEM((8, 128), F32),
-            pltpu.SemaphoreType.DMA((11,)),
+            pltpu.VMEM((2, FEAT, 128), BF16),
+            pltpu.SemaphoreType.DMA((13,)),
             pltpu.SemaphoreType.DMA((11,)),
             pltpu.SemaphoreType.DMA((8,)),
             pltpu.SemaphoreType.DMA((8,)),
+            pltpu.SemaphoreType.DMA((2,)),
+            pltpu.SemaphoreType.DMA((8,)),
+            pltpu.SemaphoreType.DMA((2,)),
         ],
         compiler_params=pltpu.CompilerParams(
-            collective_id=0, has_side_effects=True, vmem_limit_bytes=50 * 1024 * 1024
+            collective_id=0, has_side_effects=True, vmem_limit_bytes=63 * 1024 * 1024
         ),
         name="sage_layer",
     )(
@@ -448,6 +507,16 @@
         edge_target.reshape(blocks, 128),
         receive_rows.reshape(16, 128),
     )
+    act, fgrad, self_grad, mean_grad, bias_grad = pl.pallas_call(
+        hand_on,
+        out_shape=out_shape,
+        in_specs=[far] * 5,
+        out_specs=[far] * 5,
+        scratch_shapes=[pltpu.VMEM(one.shape, one.dtype) for one in out_shape]
+        + [pltpu.SemaphoreType.DMA((5,))] * 2,
+        compiler_params=pltpu.CompilerParams(vmem_limit_bytes=63 * 1024 * 1024),
+        name="hand_on",
+    )(*results)
     return act, fgrad, self_grad, mean_grad, bias_grad.reshape(WIDE)
 
 

time: 91.8 us -> 85.5 us (0.931); the launches traced: 90.7 us -> 85.3 us
  local copies, waits for them, and re-layouts: 9.23 us -> 0 us
  Pallas kernels: 80.1 us -> 84 us
    unnamed x21 -> x0, local copies, waits for them, and re-layouts: 9.23 us -> none
    pallas_call x1 -> x2, Pallas kernels: 80.1 us -> 84 us  [the longest x1 81.9 us: local(): pl.pallas_call(kernel, out_shape=out_shape, in_specs=[pl.BlockSpec(memory...]
where the time goes in v2:
time: 85.5 us; the launch traced here: 85.3 us
  Pallas kernels  84 us (98%)
  between operations  1.29 us (2%)
    pallas_call x1, Pallas kernels, local(): pl.pallas_call(kernel, out_shape=out_shape, in_specs=[pl.BlockSpec(memory...  81.9 us
    pallas_call x1, Pallas kernels, local(): pl.pallas_call(hand_on, out_shape=out_shape, in_specs=[far] * 5, out_spec...  2.09 us

profile of v2, /device:TPU:1, one launch (start us, length us, event | category | flops | bytes accessed | tf_op | source)
XLA Modules:
  0.0 85.3 jit_solution(5122109810048936185)
XLA Ops:
  1.3 81.9 %sage_layer.1 = (bf16[1024,256]{1,0:T(8,128)(2,1)}, bf16[1024,128]{1,0:T(8,128)(2,1)}, f32[128,256]{1,0:T(8,128)}, f32[128,256]{1,0:T(8,128)}, f32[1,256]{1,0:T(1,128)}) custom-call(s32[1,1]{1,0:T(1,128)S(6)} %copy.14.count_ref, bf16[1024,128]{1,0:T(8,128)(2,1)} %feat_hbm.1, bf16[1024,256]{1,0:T(8,128)(2,1)} %cot_hbm.1, bf16[128,256]{1,0:T(8,128)(2,1)} %w_self_hbm.1, ...), custom_call_target="tpu_custom_call" | custom-call | tf_op jit(solution)/shard_map/sage_layer/pallas_call | solution.py:434
  83.2 2.1 %hand_on.1 = (bf16[1024,256]{1,0:T(8,128)(2,1)}, bf16[1024,128]{1,0:T(8,128)(2,1)}, f32[128,256]{1,0:T(8,128)}, f32[128,256]{1,0:T(8,128)}, f32[1,256]{1,0:T(1,128)}) custom-call(bf16[1024,256]{1,0:T(8,128)(2,1)} %get-tuple-element.15.refs_0_, bf16[1024,128]{1,0:T(8,128)(2,1)} %get-tuple-element.16.refs_1_, f32[128,256]{1,0:T(8,128)} %get-tuple-element.17.refs_2_, ...), custom_call_target="tpu_custom_call" | custom-call | tf_op jit(solution)/shard_map/hand_on/pallas_call | solution.py:510
